TPU v7x, 32 devices: a whole 2x2x4 slice. The times are simulated.
32 devices in a mesh: grp: 2 (over x), sp: 8 (over z, y), ch: 2 (over core).
Axes of the slice: x: 2, y: 2, z: 4, core: 2. Of those that a mesh axis runs over, the one named last changes fastest.
Arguments:
- grid_tokens: bfloat16 [16, 128, 2048], P(('grp', 'sp'), None, 'ch'), parts along dimension 0, may hold values from -6 to 6
- conv_weight: float32 [3, 3, 2048], P(None, None, 'ch'), may hold values from -2 to 2
- norm_gain: float32 [2048], replicated, may hold values from 0.1 to 1.9
- qkv_weight: bfloat16 [2048, 3, 2048], P('sp', None, 'ch'), may hold values from -1 to 1
Outputs:
- attended: bfloat16 [16, 128, 2048], P(('grp', 'sp'), None, 'ch'), parts along dimension 0
There are 2 independent parts, one for each index of `grp`. A program takes and returns all parts, laid end to end along the dimension named above; an argument that names none is the same for every part. Nothing has to cross between parts.
All inputs are finite; a program needn't handle non-finite values.
Results may differ from a plain program's by a relative error of at most 0.0097.
Values may be sent and summed in bfloat16 or wider, within the bound.
A program may use at most 128 MiB of HBM per device.

v0:
```python
import jax
import jax.numpy as jnp
from jax import lax
from jax.sharding import PartitionSpec as P

D = 2048
HEAD_DIM = 64


def with_halo(block, sides, width):
    for axis, dim in sides:
        count = lax.axis_size(axis)
        forward = [(i, i + 1) for i in range(count - 1)]
        backward = [(target, source) for source, target in forward]
        low = lax.ppermute(
            lax.slice_in_dim(block, block.shape[dim] - width, None, axis=dim), axis, forward
        )
        high = lax.ppermute(lax.slice_in_dim(block, 0, width, axis=dim), axis, backward)
        block = jnp.concatenate([low, block, high], axis=dim)
    return block


def make_attend(query, heads_n):
    inv_scale = 1.0 / jnp.sqrt(jnp.float32(HEAD_DIM))

    def attend(carry, pieces, start):
        running_top, running_total, accum = carry
        key_piece, value_piece = pieces
        width = key_piece.shape[0]
        key_heads = key_piece.reshape(width, heads_n, HEAD_DIM)
        value_heads = value_piece.reshape(width, heads_n, HEAD_DIM)
        scores = (
            jnp.einsum("thd,nhd->htn", query, key_heads, preferred_element_type=jnp.float32)
            * inv_scale
        )
        new_top = jnp.maximum(running_top, jnp.max(scores, axis=2))
        expo = jnp.exp(scores - new_top[:, :, None])
        new_total = jnp.sum(expo, axis=2)
        probs = expo.astype(jnp.bfloat16)
        update = jnp.einsum("htn,nhd->htd", probs, value_heads, preferred_element_type=jnp.float32)
        return (new_top, new_total, update)

    return attend


def start_state(heads_n, queries_n):
    return (
        jnp.full((heads_n, queries_n), -1e30, jnp.float32),
        jnp.zeros((heads_n, queries_n), jnp.float32),
        jnp.zeros((heads_n, queries_n, HEAD_DIM), jnp.float32),
    )


def local(grid_tokens, conv_weight, norm_gain, qkv_weight):
    rows, cols, local_ch = grid_tokens.shape
    count = rows * cols
    heads_here = local_ch // HEAD_DIM
    extended = with_halo(grid_tokens, (("sp", 0),), 1)
    padded = jnp.pad(extended.astype(jnp.float32), ((0, 0), (1, 1), (0, 0)))
    conv = jnp.zeros((rows, cols, local_ch), jnp.float32)
    for row_off in range(3):
        for col_off in range(3):
            conv = (
                conv
                + padded[row_off : row_off + rows, col_off : col_off + cols]
                * conv_weight[row_off, col_off]
            )
    mixed = (grid_tokens.astype(jnp.float32) + conv).astype(jnp.bfloat16)
    full = lax.all_gather(mixed, "ch", axis=2, tiled=True)
    flat = full.astype(jnp.float32).reshape(count, D)
    mean = jnp.mean(flat, axis=1, keepdims=True)
    var = jnp.mean((flat - mean) ** 2, axis=1, keepdims=True)
    normed = ((flat - mean) * lax.rsqrt(var + 1e-06) * norm_gain).astype(jnp.bfloat16)
    panel = lax.all_gather(qkv_weight, "sp", axis=0, tiled=True)
    proj = jnp.dot(normed, panel.reshape(D, 3 * local_ch), preferred_element_type=jnp.float32)
    proj = proj.astype(jnp.bfloat16)
    query_local = proj[:, :local_ch]
    key_local = proj[:, local_ch : 2 * local_ch]
    value_local = proj[:, 2 * local_ch :]
    query = query_local.reshape(count, heads_here, HEAD_DIM)
    attend = make_attend(query, heads_here)
    init = start_state(heads_here, count)
    final = attend(
        init,
        (
            lax.all_gather(key_local, "sp", axis=0, tiled=True),
            lax.all_gather(value_local, "sp", axis=0, tiled=True),
        ),
        jnp.int32(0),
    )
    result = final[2] / final[1][:, :, None]
    result = result.transpose(1, 0, 2).reshape(rows, cols, local_ch)
    return result.astype(jnp.bfloat16)


def solution(mesh):
    placed = (P(("grp", "sp"), None, "ch"), P(None, None, "ch"), P(), P("sp", None, "ch"))
    return jax.shard_map(
        local, mesh=mesh, in_specs=placed, out_specs=P(("grp", "sp"), None, "ch"), check_vma=False
    )
```

profile of v0, /device:TPU:0, one launch (start us, length us, event | category | flops | bytes accessed | tf_op | source)
XLA Modules:
  0.0 317.5 jit_solution(10617285309624807875)
XLA Ops:
  6.5 0.0 copy-start.1
  6.5 0.0 all-gather.4.cloned.1.call-start
  6.5 2.6 copy.9
  9.2 0.0 all-gather.4.cloned.1.call-update
  9.2 0.0 all-gather.6.cloned.1.call-start
  9.2 1.3 collective-permute-start.1
  10.5 5.5 %collective-permute-start = (bf16[1,128,1024]{2,1,0:T(8,128)(2,1)}, bf16[1,128,1024]{2,1,0:T(8,128)(2,1)S(1)}, u32[]{:S(2)}, u32[]{:S(2)}) collective-permute-start(bf16[1,128,1024]{2,1,0:T(8,128)(2,1)} %param.4), channel_id=1, source_target_pairs={{0,2},{2,4},{4,6},{6,8},{8,10},{10,12},{12,14},{1,3},{3,5},{5,7},{... | collective-permute-start | bytes 786440 | tf_op jit(solution)/shard_map/ppermute | solution.py:15
  16.1 0.9 fusion.44
  17.0 3.6 %collective-permute-done.1 = bf16[1,128,1024]{2,1,0:T(8,128)(2,1)S(1)} collective-permute-done((bf16[1,128,1024]{2,1,0:T(8,128)(2,1)}, bf16[1,128,1024]{2,1,0:T(8,128)(2,1)S(1)}, u32[]{:S(2)}, u32[]{:S(2)}) %collective-permute-start.1) | collective-permute-done | bytes 262176 | tf_op jit(solution)/shard_map/ppermute | solution.py:18
  20.6 10.6 %collective-permute-done = bf16[1,128,1024]{2,1,0:T(8,128)(2,1)S(1)} collective-permute-done((bf16[1,128,1024]{2,1,0:T(8,128)(2,1)}, bf16[1,128,1024]{2,1,0:T(8,128)(2,1)S(1)}, u32[]{:S(2)}, u32[]{:S(2)}) %collective-permute-start) | collective-permute-done | bytes 262176 | tf_op jit(solution)/shard_map/ppermute | solution.py:15
  31.2 1.1 maximum_convert_fusion
  32.3 1.5 fusion.41
  33.8 2.2 all_gather.12
  36.0 0.2 convert_reduce_fusion
  36.1 0.3 fusion.14
  36.4 158.4 %all-gather.4.cloned.1.call-done = bf16[2048,3,1024]{0,2,1:T(8,128)(2,1)} async-done(((bf16[256,3,1024]{0,2,1:T(8,128)(2,1)}), bf16[2048,3,1024]{0,2,1:T(8,128)(2,1)}) %all-gather.4.cloned.1.call-update) | async-done | bytes 12582928 | tf_op jit(solution)/shard_map/all_gather | solution.py:74
  194.8 0.0 copy-done.1
  194.8 8.9 %convolution_convert_fusion = bf16[128,3072]{1,0:T(8,128)(2,1)S(1)} fusion(bf16[2048,3072]{0,1:T(8,128)(2,1)} %bitcast.36, bf16[1,128,2048]{2,1,0:T(8,128)(2,1)S(1)} %all_gather.12, f32[2048]{0:T(1024)S(1)} %copy-done.1, f32[128]{0:T(128)S(1)} %add_rsqrt_fusion, f32[128]{0:T(128)S(1)} %broadcast_multiply_fusion), kind=kOutput, calls=%fused_computation.7 | convolution fusion | flops 1612316672 | bytes 13902848 | tf_op jit(solution)/shard_map/dot_general | solution.py:75
  203.8 0.8 fusion.43
  204.6 0.0 all-gather.6.cloned.1.call-update
  204.6 0.0 all-gather.8.cloned.1.call-start
  204.7 0.7 all-gather.8.cloned.1.call-update
  205.4 0.2 copy.10
  205.5 46.7 %all-gather.6.cloned.1.call-done = bf16[1024,1024]{1,0:T(8,128)(2,1)} async-done(((bf16[128,1024]{1,0:T(8,128)(2,1)}), bf16[1024,1024]{1,0:T(8,128)(2,1)}) %all-gather.6.cloned.1.call-update) | async-done | bytes 2097168 | tf_op jit(solution)/shard_map/all_gather | solution.py:86
  252.2 2.9 copy.11
  255.1 1.4 multiply_reduce_fusion
  256.5 0.0 copy-start
  256.5 3.2 %copy-done = f32[16,128,1024]{2,1,0:T(8,128)} copy-done((f32[16,128,1024]{2,1,0:T(8,128)}, f32[16,128,1024]{2,1,0:T(8,128)S(1)}, u32[]{:S(2)}) %copy-start) | copy-done | bytes 8388632
  259.7 1.8 fusion
  261.5 40.7 %all-gather.8.cloned.1.call-done = bf16[1024,1024]{1,0:T(8,128)(2,1)} async-done(((bf16[128,1024]{1,0:T(8,128)(2,1)}), bf16[1024,1024]{1,0:T(8,128)(2,1)}) %all-gather.8.cloned.1.call-update) | async-done | bytes 2097168 | tf_op jit(solution)/shard_map/all_gather | solution.py:87
  302.2 2.9 copy.12
  305.0 5.1 %fusion.18 = bf16[128,16,64]{0,2,1:T(8,128)(2,1)S(1)} fusion(bf16[1024,16,64]{0,2,1:T(8,128)(2,1)S(1)} %bitcast.38, f32[16,128,1024]{2,1,0:T(8,128)} %copy-done, f32[16,128]{1,0:T(8,128)S(1)} %broadcast_maximum_fusion, f32[128,16]{0,1:T(8,128)S(1)} %bitcast.50), kind=kOutput, calls=%fused_computation.25 | convolution fusion | flops 274989056 | bytes 10764288 | tf_op jit(solution)/shard_map/htn,nhd->htd/dot_general | solution.py:40
  310.2 0.9 copy.13
  (3 shorter events, 0.0 us)
Async XLA Ops:
  6.5 188.3 %copy-start.1 = (f32[2048]{0:T(1024)S(1)}, f32[2048]{0:T(1024)}, u32[]{:S(2)}) copy-start(f32[2048]{0:T(1024)} %param.6) | copy-start | bytes 24580
  6.5 188.3 %all-gather.4.cloned.1.call-start = ((), (), s32[]{:S(2)}) async-start(), calls=%async_computation | async-start | bytes 14155776 | tf_op jit(solution)/shard_map/all_gather | solution.py:74
  9.2 243.1 %all-gather.6.cloned.1.call-start = ((), (), s32[]{:S(2)}) async-start(), calls=%async_computation.1 | async-start | bytes 2359296 | tf_op jit(solution)/shard_map/all_gather | solution.py:86
  9.2 11.4 %collective-permute-start.1 = (bf16[1,128,1024]{2,1,0:T(8,128)(2,1)}, bf16[1,128,1024]{2,1,0:T(8,128)(2,1)S(1)}, u32[]{:S(2)}, u32[]{:S(2)}) collective-permute-start(bf16[1,128,1024]{2,1,0:T(8,128)(2,1)} %param.4), channel_id=1, source_target_pairs={{2,0},{4,2},{6,4},{8,6},{10,8},{12,10},{14,12},{3,1},{5,3},{7,5},{... | collective-permute-start | bytes 786440 | tf_op jit(solution)/shard_map/ppermute | solution.py:18
  10.5 20.7 %collective-permute-start = (bf16[1,128,1024]{2,1,0:T(8,128)(2,1)}, bf16[1,128,1024]{2,1,0:T(8,128)(2,1)S(1)}, u32[]{:S(2)}, u32[]{:S(2)}) collective-permute-start(bf16[1,128,1024]{2,1,0:T(8,128)(2,1)} %param.4), channel_id=1, source_target_pairs={{0,2},{2,4},{4,6},{6,8},{8,10},{10,12},{12,14},{1,3},{3,5},{5,7},{... | collective-permute-start | bytes 786440 | tf_op jit(solution)/shard_map/ppermute | solution.py:15
  204.6 97.6 %all-gather.8.cloned.1.call-start = ((), (), s32[]{:S(2)}) async-start(), calls=%async_computation.2 | async-start | bytes 2359296 | tf_op jit(solution)/shard_map/all_gather | solution.py:87
  256.5 3.2 %copy-start = (f32[16,128,1024]{2,1,0:T(8,128)}, f32[16,128,1024]{2,1,0:T(8,128)S(1)}, u32[]{:S(2)}) copy-start(f32[16,128,1024]{2,1,0:T(8,128)S(1)} %get-tuple-element.18) | copy-start | bytes 25165828
Sparse Core Ops, SparseCore 0:
  9.4 185.3 all-gather.3
  204.7 47.4 all-gather.5
  254.4 47.7 all-gather.7
where the time goes:
time: 318 us
  waiting for transfers between devices  261 us (82%)
  matrix products  15.4 us (5%)
  local copies, waits for them, and re-layouts  14.3 us (4%)
  between operations  13.2 us (4%)
  starting transfers between devices  6.9 us (2%)
  other arithmetic  4.84 us (2%)
    all_gather x1, waiting for transfers between devices, local(): panel = lax.all_gather(qkv_weight, 'sp', axis=0, tiled=True)  158 us
    all_gather x1, waiting for transfers between devices, local(): lax.all_gather(key_local, 'sp', axis=0, tiled=True)  46.7 us
    all_gather x1, waiting for transfers between devices, local(): lax.all_gather(value_local, 'sp', axis=0, tiled=True)  40.7 us
    ppermute x1, waiting for transfers between devices, with_halo(): lax.ppermute(lax.slice_in_dim(block, block.shape[dim] - width, None, axis...  10.6 us
    dot_general x1, matrix products, local(): jnp.dot(normed, panel.reshape(D, 3 * local_ch), preferred_element_type=jn...  8.9 us
  transfers between devices with their start and end apart: 5, of which 5 were waited for; matrix products, arithmetic and copies ran while one was open for 3% of the time, Pallas kernels for 0%

commit v1 on v0

--- a/solution.py
+++ b/solution.py
@@ -1,6 +1,10 @@
+import functools
+
 import jax
 import jax.numpy as jnp
 from jax import lax
+from jax.experimental import pallas as pl
+from jax.experimental.pallas import tpu as pltpu
 from jax.sharding import PartitionSpec as P
 
 D = 2048
@@ -51,7 +55,7 @@
     )
 
 
-def local(grid_tokens, conv_weight, norm_gain, qkv_weight):
+def local_gathered(grid_tokens, conv_weight, norm_gain, qkv_weight):
     rows, cols, local_ch = grid_tokens.shape
     count = rows * cols
     heads_here = local_ch // HEAD_DIM
@@ -93,8 +97,343 @@
     return result.astype(jnp.bfloat16)
 
 
+MESH = pl.DeviceIdType.MESH
+
+
+def fused_kernel(
+    n, x_ref, conv_ref, gain_ref, w_ref, out_ref,
+    halo, mix, xs, ws, qs, ks, vs, os,
+    halo_send, halo_recv, own_sem, w_send, w_recv, f_send, f_recv, mix_send, mix_recv,
+    ring_send, ring_recv, peer_send, peer_recv, out_send, out_recv,
+):
+    tokens, local_ch = x_ref.shape
+    depth, wide = w_ref.shape[1], qs.shape[1]
+    share, half = depth // 2, n // 2
+    g, s, c = lax.axis_index("grp"), lax.axis_index("sp"), lax.axis_index("ch")
+    pos = (s % 2) * (n - 1) + (1 - 2 * (s % 2)) * (s // 2)
+
+    def at_ring(p):
+        p = lax.rem(p + 2 * n, n)
+        back = p // half
+        return 2 * (p * (1 - back) + (n - 1 - p) * back) + back
+
+    def send(src, dst, send_sem, recv_sem, to):
+        return pltpu.make_async_remote_copy(
+            src_ref=src, dst_ref=dst, send_sem=send_sem, recv_sem=recv_sem,
+            device_id=to, device_id_type=MESH,
+        )
+
+    other_group, other_core = (1 - g, s, c), (g, s, 1 - c)
+
+    barrier = pltpu.get_barrier_semaphore()
+    for k in range(1, n):
+        pl.semaphore_signal(barrier, inc=1, device_id=(g, lax.rem(s + k, n), c), device_id_type=MESH)
+    pl.semaphore_signal(barrier, inc=1, device_id=other_group, device_id_type=MESH)
+    pl.semaphore_signal(barrier, inc=1, device_id=other_core, device_id_type=MESH)
+    pl.semaphore_wait(barrier, n + 1)
+
+    def halo_down():
+        return send(x_ref, halo.at[0], halo_send.at[0], halo_recv.at[0], (g, lax.rem(s + 1, n), c))
+
+    def halo_up():
+        return send(x_ref, halo.at[1], halo_send.at[1], halo_recv.at[1], (g, lax.rem(s + n - 1, n), c))
+
+    @pl.when(s < n - 1)
+    def _():
+        halo_down().start()
+
+    @pl.when(s > 0)
+    def _():
+        halo_up().start()
+
+    def w_copy(k):
+        to = lax.rem(s + k, n)
+        cols = pl.ds(pl.multiple_of(to * wide, wide), wide)
+        return send(
+            w_ref.at[:, pl.ds(g * share, share), cols],
+            ws.at[:, pl.ds(s * depth + g * share, share), :],
+            w_send.at[k], w_recv.at[k], (g, to, c),
+        )
+
+    def w_arrived(k):
+        origin = lax.rem(s + n - k, n)
+        rows = ws.at[:, pl.ds(origin * depth + g * share, share), :]
+        return send(rows, rows, f_send.at[k], w_recv.at[k], other_group)
+
+    def w_forward(k):
+        origin = lax.rem(s + n - k, n)
+        rows = ws.at[:, pl.ds(origin * depth + g * share, share), :]
+        return send(rows, rows, f_send.at[k], f_recv.at[k], other_group)
+
+    def w_forward_in(k):
+        origin = lax.rem(s + n - k, n)
+        rows = ws.at[:, pl.ds(origin * depth + (1 - g) * share, share), :]
+        return send(rows, rows, f_send.at[k], f_recv.at[k], other_group)
+
+    own_w = pltpu.make_async_copy(
+        w_ref.at[:, :, pl.ds(pl.multiple_of(s * wide, wide), wide)],
+        ws.at[:, pl.ds(s * depth, depth), :],
+        own_sem,
+    )
+    own_w.start()
+
+    def start_w(k, _):
+        w_copy(k).start()
+        return 0
+
+    lax.fori_loop(1, n, start_w, 0)
+
+    @pl.when(s > 0)
+    def _():
+        halo_down().wait_recv()
+
+    @pl.when(s == 0)
+    def _():
+        halo[0] = jnp.zeros((tokens, local_ch), jnp.bfloat16)
+
+    @pl.when(s < n - 1)
+    def _():
+        halo_up().wait_recv()
+
+    @pl.when(s == n - 1)
+    def _():
+        halo[1] = jnp.zeros((tokens, local_ch), jnp.bfloat16)
+
+    def conv_part(i, _):
+        cols = pl.ds(pl.multiple_of(i * 128, 128), 128)
+        above = halo[0, :, cols].astype(jnp.float32)
+        here = x_ref[:, cols].astype(jnp.float32)
+        below = halo[1, :, cols].astype(jnp.float32)
+        weight = conv_ref[:, :, cols]
+
+        def column(b):
+            return above * weight[0, b : b + 1] + here * weight[1, b : b + 1] + below * weight[2, b : b + 1]
+
+        token = lax.broadcasted_iota(jnp.int32, (tokens, 128), 0)
+        left = jnp.where(token == 0, 0.0, pltpu.roll(column(0), 1, 0))
+        right = jnp.where(token == tokens - 1, 0.0, pltpu.roll(column(2), tokens - 1, 0))
+        mix[c, :, cols] = (here + (left + column(1) + right)).astype(jnp.bfloat16)
+        return 0
+
+    lax.fori_loop(0, local_ch // 128, conv_part, 0)
+
+    to_peer = send(mix.at[c], mix.at[c], mix_send, mix_recv, other_core)
+    to_peer.start()
+    send(mix.at[1 - c], mix.at[1 - c], mix_send, mix_recv, other_core).wait_recv()
+
+    def norm_part(i, _):
+        rows = pl.ds(pl.multiple_of(i * 16, 16), 16)
+        first = mix[0, rows, :].astype(jnp.float32)
+        second = mix[1, rows, :].astype(jnp.float32)
+        channels = 2 * local_ch
+        mean = (jnp.sum(first, axis=1, keepdims=True) + jnp.sum(second, axis=1, keepdims=True)) / channels
+        first, second = first - mean, second - mean
+        var = (
+            jnp.sum(first * first, axis=1, keepdims=True) + jnp.sum(second * second, axis=1, keepdims=True)
+        ) / channels
+        scale = lax.rsqrt(var + 1e-06)
+        xs[s, 0, rows, :] = (first * scale * gain_ref[:, :local_ch]).astype(jnp.bfloat16)
+        xs[s, 1, rows, :] = (second * scale * gain_ref[:, local_ch:]).astype(jnp.bfloat16)
+        return 0
+
+    lax.fori_loop(0, tokens // 16, norm_part, 0)
+
+    def ring_block(way, k):
+        owner = at_ring(pos - k if way == 0 else pos + k)
+        if k < half:
+            return xs.at[owner, c]
+        return xs.at[owner, c, pl.ds(way * (tokens // 2), tokens // 2)]
+
+    def ring_copy(way, k):
+        owner = at_ring(pos - (k - 1) if way == 0 else pos + (k - 1))
+        part = xs.at[owner, c] if k < half else xs.at[owner, c, pl.ds(way * (tokens // 2), tokens // 2)]
+        to = (g, at_ring(pos + 1 if way == 0 else pos - 1), c)
+        return send(part, part, ring_send.at[way, k], ring_recv.at[way, k], to)
+
+    def ring_arrived(way, k):
+        part = ring_block(way, k)
+        return send(part, part, ring_send.at[way, k], ring_recv.at[way, k], other_core)
+
+    def peer_copy(way, k):
+        part = ring_block(way, k)
+        return send(part, part, peer_send.at[way, k], peer_recv.at[way, k], other_core)
+
+    def peer_arrived(way, k):
+        owner = at_ring(pos - k if way == 0 else pos + k)
+        part = xs.at[owner, 1 - c]
+        if k == half:
+            part = xs.at[owner, 1 - c, pl.ds(way * (tokens // 2), tokens // 2)]
+        return send(part, part, peer_send.at[way, k], peer_recv.at[way, k], other_core)
+
+    def project(owner):
+        total = []
+        for lo, hi in ((0, 1), (1, 3)):
+            value = jnp.zeros((tokens, (hi - lo) * wide), jnp.float32)
+            for h in range(2):
+                weight = jnp.concatenate([ws[j, h * local_ch : (h + 1) * local_ch] for j in range(lo, hi)], axis=1)
+                value = value + jnp.dot(xs[owner, h], weight, preferred_element_type=jnp.float32)
+            total.append(value)
+        rows = pl.ds(pl.multiple_of(owner * tokens, tokens), tokens)
+        qs[rows, :] = total[0].astype(jnp.bfloat16)
+        ks[rows, :] = total[1][:, :wide].astype(jnp.bfloat16)
+        vs[rows, :] = total[1][:, wide:].astype(jnp.bfloat16)
+
+    def project_pair(k):
+        def one(i, _):
+            project(at_ring(pos - k + 2 * k * i))
+            return 0
+
+        lax.fori_loop(0, 2, one, 0)
+
+    for way in range(2):
+        ring_copy(way, 1).start()
+
+    def forward_w(k, _):
+        w_arrived(k).wait_recv()
+        w_forward(k).start()
+        return 0
+
+    lax.fori_loop(1, n, forward_w, 0)
+
+    for k in range(1, half + 1):
+        for way in range(2):
+            ring_arrived(way, k).wait_recv()
+            if k < half:
+                ring_copy(way, k + 1).start()
+            peer_copy(way, k).start()
+        if k == 1:
+            own_w.wait()
+
+            def w_last(j, _):
+                w_forward_in(j).wait_recv()
+                return 0
+
+            lax.fori_loop(1, n, w_last, 0)
+            project(s)
+        else:
+            for way in range(2):
+                peer_arrived(way, k - 1).wait_recv()
+            project_pair(k - 1)
+    for way in range(2):
+        peer_arrived(way, half).wait_recv()
+    project(at_ring(pos + half))
+
+    def out_copy(i):
+        to = lax.rem(s + 1 + i, n)
+        return send(
+            os.at[i], out_ref.at[:, pl.ds(pl.multiple_of(s * wide, wide), wide)],
+            out_send.at[i], out_recv.at[i], (g, to, c),
+        )
+
+    def out_arrived(i):
+        origin = lax.rem(s + 2 * n - 1 - i, n)
+        return send(
+            os.at[i], out_ref.at[:, pl.ds(pl.multiple_of(origin * wide, wide), wide)],
+            out_send.at[i], out_recv.at[i], other_core,
+        )
+
+    heads = wide // HEAD_DIM
+
+    def attend_block(i, _):
+        block = lax.rem(s + 1 + i, n)
+        query = qs[pl.ds(pl.multiple_of(block * tokens, tokens), tokens), :]
+        lane = lax.broadcasted_iota(jnp.int32, (tokens, wide), 1) // HEAD_DIM
+        result = jnp.zeros((tokens, wide), jnp.float32)
+        for h in range(heads):
+            own = jnp.where(lane == h, query.astype(jnp.float32) * HEAD_DIM**-0.5, 0.0).astype(jnp.bfloat16)
+            scores = lax.dot_general(
+                own, ks[...], (((1,), (1,)), ((), ())), preferred_element_type=jnp.float32
+            )
+            top = jnp.max(scores, axis=1, keepdims=True)
+            expo = jnp.exp(scores - top)
+            total = jnp.sum(expo, axis=1, keepdims=True)
+            part = jnp.dot(expo.astype(jnp.bfloat16), vs[...], preferred_element_type=jnp.float32)
+            result = jnp.where(lane == h, part / total, result)
+        os[i] = result.astype(jnp.bfloat16)
+
+        @pl.when(i < n - 1)
+        def _():
+            out_copy(i).start()
+
+        return 0
+
+    lax.fori_loop(0, n, attend_block, 0)
+    out_ref[:, pl.ds(pl.multiple_of(s * wide, wide), wide)] = os[n - 1]
+
+    @pl.when(s < n - 1)
+    def _():
+        halo_down().wait_send()
+
+    @pl.when(s > 0)
+    def _():
+        halo_up().wait_send()
+
+    def sent_w(k, _):
+        w_copy(k).wait_send()
+        w_forward(k).wait_send()
+        return 0
+
+    lax.fori_loop(1, n, sent_w, 0)
+    to_peer.wait_send()
+    for k in range(1, half + 1):
+        for way in range(2):
+            ring_copy(way, k).wait_send()
+            peer_copy(way, k).wait_send()
+
+    def out_done(i, _):
+        out_copy(i).wait_send()
+        out_arrived(i).wait_recv()
+        return 0
+
+    lax.fori_loop(0, n - 1, out_done, 0)
+
+
+def local_fused(n, grid_tokens, conv_weight, norm_gain, qkv_weight):
+    rows, cols, local_ch = grid_tokens.shape
+    depth = qkv_weight.shape[0]
+    wide = local_ch // n
+    count = n * cols
+    dma = pltpu.SemaphoreType.DMA
+    vmem = pl.BlockSpec(memory_space=pltpu.VMEM)
+    half = n // 2
+    out = pl.pallas_call(
+        functools.partial(fused_kernel, n),
+        out_shape=jax.ShapeDtypeStruct((cols, local_ch), jnp.bfloat16),
+        in_specs=[vmem, vmem, vmem, pl.BlockSpec(memory_space=pl.ANY)],
+        out_specs=vmem,
+        scratch_shapes=[
+            pltpu.VMEM((2, cols, local_ch), jnp.bfloat16),
+            pltpu.VMEM((2, cols, local_ch), jnp.bfloat16),
+            pltpu.VMEM((n, 2, cols, local_ch), jnp.bfloat16),
+            pltpu.VMEM((3, n * depth, wide), jnp.bfloat16),
+            pltpu.VMEM((count, wide), jnp.bfloat16),
+            pltpu.VMEM((count, wide), jnp.bfloat16),
+            pltpu.VMEM((count, wide), jnp.bfloat16),
+            pltpu.VMEM((n, cols, wide), jnp.bfloat16),
+            dma((2,)), dma((2,)), dma, dma((n,)), dma((n,)), dma((n,)), dma((n,)), dma, dma,
+            dma((2, half + 1)), dma((2, half + 1)), dma((2, half + 1)), dma((2, half + 1)),
+            dma((n,)), dma((n,)),
+        ],
+        compiler_params=pltpu.CompilerParams(
+            collective_id=0, has_side_effects=True, vmem_limit_bytes=40 * 1024 * 1024
+        ),
+    )(
+        grid_tokens.reshape(cols, local_ch), conv_weight, norm_gain.reshape(1, D),
+        qkv_weight.transpose(1, 0, 2),
+    )
+    return out.reshape(rows, cols, local_ch)
+
+
 def solution(mesh):
     placed = (P(("grp", "sp"), None, "ch"), P(None, None, "ch"), P(), P("sp", None, "ch"))
+    groups, n, cores = mesh.shape["grp"], mesh.shape["sp"], mesh.shape["ch"]
+
+    def local(grid_tokens, conv_weight, norm_gain, qkv_weight):
+        rows, _, local_ch = grid_tokens.shape
+        if groups == 2 and cores == 2 and n % 4 == 0 and rows == 1 and local_ch == 128 * n:
+            return local_fused(n, grid_tokens, conv_weight, norm_gain, qkv_weight)
+        return local_gathered(grid_tokens, conv_weight, norm_gain, qkv_weight)
+
     return jax.shard_map(
         local, mesh=mesh, in_specs=placed, out_specs=P(("grp", "sp"), None, "ch"), check_vma=False
     )

time: 318 us -> 73.6 us (0.23)
  waiting for transfers between devices: 261 us -> 0 us
  Pallas kernels: 0 us -> 68.7 us
  matrix products: 15.4 us -> 0 us
  between operations: 13.2 us -> 0.01 us
  local copies, waits for them, and re-layouts: 14.3 us -> 4.56 us
  starting transfers between devices: 6.9 us -> 0 us
  other arithmetic: 4.84 us -> 0 us
    all_gather x3 -> x0, waiting for transfers between devices: 246 us -> none  [the longest x1 158 us: local(): panel = lax.all_gather(qkv_weight, 'sp', axis=0, tiled=True)]
    pallas_call x0 -> x1, Pallas kernels: none -> 68.7 us  [local_fused(): pl.pallas_call(functools.partial(fused_kernel, n), out_shape=jax.ShapeDty...]
    dot_general x3 -> x0, matrix products: 15.4 us -> none  [the longest x1 8.9 us: local(): jnp.dot(normed, panel.reshape(D, 3 * local_ch), preferred_element_type=jn...]
    ppermute x2 -> x0, waiting for transfers between devices: 14.2 us -> none  [the longest x1 10.6 us: with_halo(): lax.ppermute(lax.slice_in_dim(block, block.shape[dim] - width, None, axis...]
    ppermute x2 -> x0, starting transfers between devices: 6.81 us -> none  [the longest x1 5.52 us: with_halo(): lax.ppermute(lax.slice_in_dim(block, block.shape[dim] - width, None, axis...]
    all_gather x2 -> x0, local copies, waits for them, and re-layouts: 5.71 us -> none  [the longest x1 2.85 us: local(): lax.all_gather(key_local, 'sp', axis=0, tiled=True)]
  transfers between devices with their start and end apart: 5 -> 0, of which waited for: 5 -> 0; matrix products, arithmetic and copies ran while one was open for 3% -> 0% of each run, Pallas kernels for 0% -> 0%
where the time goes in v1:
time: 73.6 us; the launch traced here: 73.3 us
  Pallas kernels  68.7 us (93%)
  local copies, waits for them, and re-layouts  4.56 us (6%)
    pallas_call x1, Pallas kernels, local_fused(): pl.pallas_call(functools.partial(fused_kernel, n), out_shape=jax.ShapeDty...  68.7 us
    unnamed x9, local copies, waits for them, and re-layouts  4.56 us

profile of v1, /device:TPU:0, one launch (start us, length us, event | category | flops | bytes accessed | tf_op | source)
XLA Modules:
  0.0 73.3 jit_solution(7354529393791842719)
XLA Ops:
  0.0 0.0 copy-start
  0.0 1.4 %copy-done = bf16[256,3,1024]{2,0,1:T(8,128)(2,1)S(1)} copy-done((bf16[256,3,1024]{2,0,1:T(8,128)(2,1)S(1)}, bf16[256,3,1024]{2,0,1:T(8,128)(2,1)}, u32[]{:S(2)}) %copy-start) | copy-done | bytes 1572888
  1.4 0.0 copy-start.1
  1.4 0.9 %copy-done.1 = bf16[1,128,1024]{2,1,0:T(8,128)(2,1)S(1)} copy-done((bf16[1,128,1024]{2,1,0:T(8,128)(2,1)S(1)}, bf16[1,128,1024]{2,1,0:T(8,128)(2,1)}, u32[]{:S(2)}) %copy-start.1) | copy-done | bytes 262168
  2.4 0.0 copy-start.2
  2.4 0.8 %copy-done.2 = f32[3,3,1024]{2,1,0:T(4,128)S(1)} copy-done((f32[3,3,1024]{2,1,0:T(4,128)S(1)}, f32[3,3,1024]{2,1,0:T(4,128)}, u32[]{:S(2)}) %copy-start.2) | copy-done | bytes 36888
  3.2 0.0 copy-start.3
  3.2 0.7 copy-done.3
  3.9 68.7 %shard_map.46 = bf16[128,1024]{1,0:T(8,128)(2,1)S(1)} custom-call(bf16[128,1024]{1,0:T(8,128)(2,1)S(1)} %bitcast.6, f32[3,3,1024]{2,1,0:T(4,128)S(1)} %copy-done.2, f32[1,2048]{1,0:T(1,128)S(1)} %bitcast.7, bf16[3,256,1024]{2,1,0:T(8,128)(2,1)S(1)} %bitcast.4), custom_call_target="tpu_custom_call" | custom-call | tf_op jit(solution)/shard_map/pallas_call | solution.py:399
  72.6 0.7 copy.6
Async XLA Ops:
  0.0 1.4 %copy-start = (bf16[256,3,1024]{2,0,1:T(8,128)(2,1)S(1)}, bf16[256,3,1024]{2,0,1:T(8,128)(2,1)}, u32[]{:S(2)}) copy-start(bf16[256,3,1024]{2,0,1:T(8,128)(2,1)} %param.7) | copy-start | bytes 4718596
  1.4 0.9 %copy-start.1 = (bf16[1,128,1024]{2,1,0:T(8,128)(2,1)S(1)}, bf16[1,128,1024]{2,1,0:T(8,128)(2,1)}, u32[]{:S(2)}) copy-start(bf16[1,128,1024]{2,1,0:T(8,128)(2,1)} %param.4) | copy-start | bytes 786436
  2.4 0.8 %copy-start.2 = (f32[3,3,1024]{2,1,0:T(4,128)S(1)}, f32[3,3,1024]{2,1,0:T(4,128)}, u32[]{:S(2)}) copy-start(f32[3,3,1024]{2,1,0:T(4,128)} %conv_ref.1) | copy-start | bytes 110596
  3.2 0.7 copy-start.3

commit v2 on v1

--- a/solution.py
+++ b/solution.py
@@ -103,7 +103,7 @@
 def fused_kernel(
     n, x_ref, conv_ref, gain_ref, w_ref, out_ref,
     halo, mix, xs, ws, qs, ks, vs, os,
-    halo_send, halo_recv, own_sem, w_send, w_recv, f_send, f_recv, mix_send, mix_recv,
+    halo_send, halo_recv, own_sem, w_send, w_recv, f_send, f_recv,
     ring_send, ring_recv, peer_send, peer_recv, out_send, out_recv,
 ):
     tokens, local_ch = x_ref.shape
@@ -132,19 +132,32 @@
     pl.semaphore_signal(barrier, inc=1, device_id=other_core, device_id_type=MESH)
     pl.semaphore_wait(barrier, n + 1)
 
-    def halo_down():
-        return send(x_ref, halo.at[0], halo_send.at[0], halo_recv.at[0], (g, lax.rem(s + 1, n), c))
-
-    def halo_up():
-        return send(x_ref, halo.at[1], halo_send.at[1], halo_recv.at[1], (g, lax.rem(s + n - 1, n), c))
-
-    @pl.when(s < n - 1)
-    def _():
-        halo_down().start()
-
-    @pl.when(s > 0)
-    def _():
-        halo_up().start()
+    part = local_ch // 2
+
+    def chunk(q):
+        return pl.ds(q * part, part)
+
+    def halo_down(q):
+        return send(
+            x_ref.at[:, chunk(q)], halo.at[0, :, chunk(q)], halo_send.at[0, q], halo_recv.at[0, q],
+            (g, lax.rem(s + 1, n), c),
+        )
+
+    def halo_up(q):
+        return send(
+            x_ref.at[:, chunk(q)], halo.at[1, :, chunk(q)], halo_send.at[1, q], halo_recv.at[1, q],
+            (g, lax.rem(s + n - 1, n), c),
+        )
+
+    for q in range(2):
+
+        @pl.when(s < n - 1)
+        def _():
+            halo_down(q).start()
+
+        @pl.when(s > 0)
+        def _():
+            halo_up(q).start()
 
     def w_copy(k):
         to = lax.rem(s + k, n)
@@ -183,17 +196,9 @@
 
     lax.fori_loop(1, n, start_w, 0)
 
-    @pl.when(s > 0)
-    def _():
-        halo_down().wait_recv()
-
     @pl.when(s == 0)
     def _():
         halo[0] = jnp.zeros((tokens, local_ch), jnp.bfloat16)
-
-    @pl.when(s < n - 1)
-    def _():
-        halo_up().wait_recv()
 
     @pl.when(s == n - 1)
     def _():
@@ -212,66 +217,74 @@
         token = lax.broadcasted_iota(jnp.int32, (tokens, 128), 0)
         left = jnp.where(token == 0, 0.0, pltpu.roll(column(0), 1, 0))
         right = jnp.where(token == tokens - 1, 0.0, pltpu.roll(column(2), tokens - 1, 0))
-        mix[c, :, cols] = (here + (left + column(1) + right)).astype(jnp.bfloat16)
-        return 0
-
-    lax.fori_loop(0, local_ch // 128, conv_part, 0)
-
-    to_peer = send(mix.at[c], mix.at[c], mix_send, mix_recv, other_core)
-    to_peer.start()
-    send(mix.at[1 - c], mix.at[1 - c], mix_send, mix_recv, other_core).wait_recv()
-
-    def norm_part(i, _):
-        rows = pl.ds(pl.multiple_of(i * 16, 16), 16)
-        first = mix[0, rows, :].astype(jnp.float32)
-        second = mix[1, rows, :].astype(jnp.float32)
-        channels = 2 * local_ch
-        mean = (jnp.sum(first, axis=1, keepdims=True) + jnp.sum(second, axis=1, keepdims=True)) / channels
-        first, second = first - mean, second - mean
-        var = (
-            jnp.sum(first * first, axis=1, keepdims=True) + jnp.sum(second * second, axis=1, keepdims=True)
-        ) / channels
-        scale = lax.rsqrt(var + 1e-06)
-        xs[s, 0, rows, :] = (first * scale * gain_ref[:, :local_ch]).astype(jnp.bfloat16)
-        xs[s, 1, rows, :] = (second * scale * gain_ref[:, local_ch:]).astype(jnp.bfloat16)
-        return 0
-
-    lax.fori_loop(0, tokens // 16, norm_part, 0)
-
-    def ring_block(way, k):
+        xs[s, c, :, cols] = (here + (left + column(1) + right)).astype(jnp.bfloat16)
+        return 0
+
+    def norm(owner):
+        def norm_part(i, _):
+            rows = pl.ds(pl.multiple_of(i * 16, 16), 16)
+            first = xs[owner, 0, rows, :].astype(jnp.float32)
+            second = xs[owner, 1, rows, :].astype(jnp.float32)
+            channels = 2 * local_ch
+            mean = (jnp.sum(first, axis=1, keepdims=True) + jnp.sum(second, axis=1, keepdims=True)) / channels
+            first, second = first - mean, second - mean
+            var = (
+                jnp.sum(first * first, axis=1, keepdims=True) + jnp.sum(second * second, axis=1, keepdims=True)
+            ) / channels
+            scale = lax.rsqrt(var + 1e-06)
+            mix[0, rows, :] = (first * scale * gain_ref[:, :local_ch]).astype(jnp.bfloat16)
+            mix[1, rows, :] = (second * scale * gain_ref[:, local_ch:]).astype(jnp.bfloat16)
+            return 0
+
+        lax.fori_loop(0, tokens // 16, norm_part, 0)
+
+    def pieces(way, k):
+        return (0, 1) if k < half else (way,)
+
+    def block(way, k, q, core):
         owner = at_ring(pos - k if way == 0 else pos + k)
-        if k < half:
-            return xs.at[owner, c]
-        return xs.at[owner, c, pl.ds(way * (tokens // 2), tokens // 2)]
-
-    def ring_copy(way, k):
-        owner = at_ring(pos - (k - 1) if way == 0 else pos + (k - 1))
-        part = xs.at[owner, c] if k < half else xs.at[owner, c, pl.ds(way * (tokens // 2), tokens // 2)]
+        return xs.at[owner, core, :, chunk(q)]
+
+    def ring_copy(way, k, q):
+        piece = block(way, k - 1, q, c)
         to = (g, at_ring(pos + 1 if way == 0 else pos - 1), c)
-        return send(part, part, ring_send.at[way, k], ring_recv.at[way, k], to)
-
-    def ring_arrived(way, k):
-        part = ring_block(way, k)
-        return send(part, part, ring_send.at[way, k], ring_recv.at[way, k], other_core)
-
-    def peer_copy(way, k):
-        part = ring_block(way, k)
-        return send(part, part, peer_send.at[way, k], peer_recv.at[way, k], other_core)
-
-    def peer_arrived(way, k):
-        owner = at_ring(pos - k if way == 0 else pos + k)
-        part = xs.at[owner, 1 - c]
-        if k == half:
-            part = xs.at[owner, 1 - c, pl.ds(way * (tokens // 2), tokens // 2)]
-        return send(part, part, peer_send.at[way, k], peer_recv.at[way, k], other_core)
+        return send(piece, piece, ring_send.at[way, k, q], ring_recv.at[way, k, q], to)
+
+    def ring_arrived(way, k, q):
+        piece = block(way, k, q, c)
+        return send(piece, piece, ring_send.at[way, k, q], ring_recv.at[way, k, q], other_core)
+
+    def peer_copy(way, k, q):
+        piece = block(way, k, q, c)
+        return send(piece, piece, peer_send.at[way, k, q], peer_recv.at[way, k, q], other_core)
+
+    def peer_arrived(way, k, q):
+        piece = block(way, k, q, 1 - c)
+        return send(piece, piece, peer_send.at[way, k, q], peer_recv.at[way, k, q], other_core)
+
+    for q in range(2):
+
+        @pl.when(s > 0)
+        def _():
+            halo_down(q).wait_recv()
+
+        @pl.when(s < n - 1)
+        def _():
+            halo_up(q).wait_recv()
+
+        lax.fori_loop(q * (part // 128), (q + 1) * (part // 128), conv_part, 0)
+        for way in range(2):
+            ring_copy(way, 1, q).start()
+        peer_copy(0, 0, q).start()
 
     def project(owner):
+        norm(owner)
         total = []
         for lo, hi in ((0, 1), (1, 3)):
             value = jnp.zeros((tokens, (hi - lo) * wide), jnp.float32)
             for h in range(2):
                 weight = jnp.concatenate([ws[j, h * local_ch : (h + 1) * local_ch] for j in range(lo, hi)], axis=1)
-                value = value + jnp.dot(xs[owner, h], weight, preferred_element_type=jnp.float32)
+                value = value + jnp.dot(mix[h], weight, preferred_element_type=jnp.float32)
             total.append(value)
         rows = pl.ds(pl.multiple_of(owner * tokens, tokens), tokens)
         qs[rows, :] = total[0].astype(jnp.bfloat16)
@@ -285,9 +298,6 @@
 
         lax.fori_loop(0, 2, one, 0)
 
-    for way in range(2):
-        ring_copy(way, 1).start()
-
     def forward_w(k, _):
         w_arrived(k).wait_recv()
         w_forward(k).start()
@@ -296,11 +306,13 @@
     lax.fori_loop(1, n, forward_w, 0)
 
     for k in range(1, half + 1):
-        for way in range(2):
-            ring_arrived(way, k).wait_recv()
-            if k < half:
-                ring_copy(way, k + 1).start()
-            peer_copy(way, k).start()
+        for q in range(2):
+            for way in range(2):
+                if q in pieces(way, k):
+                    ring_arrived(way, k, q).wait_recv()
+                    if k < half and q in pieces(way, k + 1):
+                        ring_copy(way, k + 1, q).start()
+                    peer_copy(way, k, q).start()
         if k == 1:
             own_w.wait()
 
@@ -309,13 +321,16 @@
                 return 0
 
             lax.fori_loop(1, n, w_last, 0)
+            for q in range(2):
+                peer_arrived(0, 0, q).wait_recv()
             project(s)
         else:
             for way in range(2):
-                peer_arrived(way, k - 1).wait_recv()
+                for q in range(2):
+                    peer_arrived(way, k - 1, q).wait_recv()
             project_pair(k - 1)
     for way in range(2):
-        peer_arrived(way, half).wait_recv()
+        peer_arrived(way, half, way).wait_recv()
     project(at_ring(pos + half))
 
     def out_copy(i):
@@ -335,8 +350,8 @@
     heads = wide // HEAD_DIM
 
     def attend_block(i, _):
-        block = lax.rem(s + 1 + i, n)
-        query = qs[pl.ds(pl.multiple_of(block * tokens, tokens), tokens), :]
+        target = lax.rem(s + 1 + i, n)
+        query = qs[pl.ds(pl.multiple_of(target * tokens, tokens), tokens), :]
         lane = lax.broadcasted_iota(jnp.int32, (tokens, wide), 1) // HEAD_DIM
         result = jnp.zeros((tokens, wide), jnp.float32)
         for h in range(heads):
@@ -360,13 +375,15 @@
     lax.fori_loop(0, n, attend_block, 0)
     out_ref[:, pl.ds(pl.multiple_of(s * wide, wide), wide)] = os[n - 1]
 
-    @pl.when(s < n - 1)
-    def _():
-        halo_down().wait_send()
-
-    @pl.when(s > 0)
-    def _():
-        halo_up().wait_send()
+    for q in range(2):
+
+        @pl.when(s < n - 1)
+        def _():
+            halo_down(q).wait_send()
+
+        @pl.when(s > 0)
+        def _():
+            halo_up(q).wait_send()
 
     def sent_w(k, _):
         w_copy(k).wait_send()
@@ -374,11 +391,13 @@
         return 0
 
     lax.fori_loop(1, n, sent_w, 0)
-    to_peer.wait_send()
+    for q in range(2):
+        peer_copy(0, 0, q).wait_send()
     for k in range(1, half + 1):
         for way in range(2):
-            ring_copy(way, k).wait_send()
-            peer_copy(way, k).wait_send()
+            for q in pieces(way, k):
+                ring_copy(way, k, q).wait_send()
+                peer_copy(way, k, q).wait_send()
 
     def out_done(i, _):
         out_copy(i).wait_send()
@@ -410,8 +429,8 @@
             pltpu.VMEM((count, wide), jnp.bfloat16),
             pltpu.VMEM((count, wide), jnp.bfloat16),
             pltpu.VMEM((n, cols, wide), jnp.bfloat16),
-            dma((2,)), dma((2,)), dma, dma((n,)), dma((n,)), dma((n,)), dma((n,)), dma, dma,
-            dma((2, half + 1)), dma((2, half + 1)), dma((2, half + 1)), dma((2, half + 1)),
+            dma((2, 2)), dma((2, 2)), dma, dma((n,)), dma((n,)), dma((n,)), dma((n,)),
+            dma((2, half + 1, 2)), dma((2, half + 1, 2)), dma((2, half + 1, 2)), dma((2, half + 1, 2)),
             dma((n,)), dma((n,)),
         ],
         compiler_params=pltpu.CompilerParams(

time: 73.6 us -> 78.3 us (1.064)
  Pallas kernels: 68.7 us -> 73.4 us
    pallas_call x1, Pallas kernels: 68.7 us -> 73.4 us  [local_fused(): pl.pallas_call(functools.partial(fused_kernel, n), out_shape=jax.ShapeDty...]
where the time goes in v2:
time: 78.3 us; the launch traced here: 78 us
  Pallas kernels  73.4 us (94%)
  local copies, waits for them, and re-layouts  4.56 us (6%)
    pallas_call x1, Pallas kernels, local_fused(): pl.pallas_call(functools.partial(fused_kernel, n), out_shape=jax.ShapeDty...  73.4 us
    unnamed x9, local copies, waits for them, and re-layouts  4.56 us

profile of v2, /device:TPU:0, one launch (start us, length us, event | category | flops | bytes accessed | tf_op | source)
XLA Modules:
  0.0 78.0 jit_solution(16452576200287208250)
XLA Ops:
  0.0 0.0 copy-start
  0.0 1.4 %copy-done = bf16[256,3,1024]{2,0,1:T(8,128)(2,1)S(1)} copy-done((bf16[256,3,1024]{2,0,1:T(8,128)(2,1)S(1)}, bf16[256,3,1024]{2,0,1:T(8,128)(2,1)}, u32[]{:S(2)}) %copy-start) | copy-done | bytes 1572888
  1.4 0.0 copy-start.1
  1.4 0.9 %copy-done.1 = bf16[1,128,1024]{2,1,0:T(8,128)(2,1)S(1)} copy-done((bf16[1,128,1024]{2,1,0:T(8,128)(2,1)S(1)}, bf16[1,128,1024]{2,1,0:T(8,128)(2,1)}, u32[]{:S(2)}) %copy-start.1) | copy-done | bytes 262168
  2.4 0.0 copy-start.2
  2.4 0.8 %copy-done.2 = f32[3,3,1024]{2,1,0:T(4,128)S(1)} copy-done((f32[3,3,1024]{2,1,0:T(4,128)S(1)}, f32[3,3,1024]{2,1,0:T(4,128)}, u32[]{:S(2)}) %copy-start.2) | copy-done | bytes 36888
  3.2 0.0 copy-start.3
  3.2 0.7 copy-done.3
  3.9 73.4 %shard_map.46 = bf16[128,1024]{1,0:T(8,128)(2,1)S(1)} custom-call(bf16[128,1024]{1,0:T(8,128)(2,1)S(1)} %bitcast.6, f32[3,3,1024]{2,1,0:T(4,128)S(1)} %copy-done.2, f32[1,2048]{1,0:T(1,128)S(1)} %bitcast.7, bf16[3,256,1024]{2,1,0:T(8,128)(2,1)S(1)} %bitcast.4), custom_call_target="tpu_custom_call" | custom-call | tf_op jit(solution)/shard_map/pallas_call | solution.py:418
  77.3 0.7 copy.6
Async XLA Ops:
  0.0 1.4 %copy-start = (bf16[256,3,1024]{2,0,1:T(8,128)(2,1)S(1)}, bf16[256,3,1024]{2,0,1:T(8,128)(2,1)}, u32[]{:S(2)}) copy-start(bf16[256,3,1024]{2,0,1:T(8,128)(2,1)} %param.7) | copy-start | bytes 4718596
  1.4 0.9 %copy-start.1 = (bf16[1,128,1024]{2,1,0:T(8,128)(2,1)S(1)}, bf16[1,128,1024]{2,1,0:T(8,128)(2,1)}, u32[]{:S(2)}) copy-start(bf16[1,128,1024]{2,1,0:T(8,128)(2,1)} %param.4) | copy-start | bytes 786436
  2.4 0.8 %copy-start.2 = (f32[3,3,1024]{2,1,0:T(4,128)S(1)}, f32[3,3,1024]{2,1,0:T(4,128)}, u32[]{:S(2)}) copy-start(f32[3,3,1024]{2,1,0:T(4,128)} %conv_ref.1) | copy-start | bytes 110596
  3.2 0.7 copy-start.3

commit v3 on v1

--- a/solution.py
+++ b/solution.py
@@ -101,9 +101,9 @@
 
 
 def fused_kernel(
-    n, x_ref, conv_ref, gain_ref, w_ref, out_ref,
-    halo, mix, xs, ws, qs, ks, vs, os,
-    halo_send, halo_recv, own_sem, w_send, w_recv, f_send, f_recv, mix_send, mix_recv,
+    n, x_ref, conv_in, gain_in, w_ref, out_ref,
+    conv_ref, gain_ref, in_sem, raw, stats, xs, ws, qs, ks, vs, os,
+    own_sem, w_send, w_recv, f_send, f_recv, stat_send, stat_recv,
     ring_send, ring_recv, peer_send, peer_recv, out_send, out_recv,
 ):
     tokens, local_ch = x_ref.shape
@@ -125,26 +125,21 @@
 
     other_group, other_core = (1 - g, s, c), (g, s, 1 - c)
 
+    own_x = pltpu.make_async_copy(x_ref, raw.at[s + 1], in_sem.at[0])
+    own_conv = pltpu.make_async_copy(conv_in, conv_ref, in_sem.at[1])
+    own_gain = pltpu.make_async_copy(gain_in, gain_ref, in_sem.at[2])
+    own_x.start()
+    own_conv.start()
+    own_gain.start()
+    raw[0] = jnp.zeros((tokens, local_ch), jnp.bfloat16)
+    raw[n + 1] = jnp.zeros((tokens, local_ch), jnp.bfloat16)
+
     barrier = pltpu.get_barrier_semaphore()
     for k in range(1, n):
         pl.semaphore_signal(barrier, inc=1, device_id=(g, lax.rem(s + k, n), c), device_id_type=MESH)
     pl.semaphore_signal(barrier, inc=1, device_id=other_group, device_id_type=MESH)
     pl.semaphore_signal(barrier, inc=1, device_id=other_core, device_id_type=MESH)
     pl.semaphore_wait(barrier, n + 1)
-
-    def halo_down():
-        return send(x_ref, halo.at[0], halo_send.at[0], halo_recv.at[0], (g, lax.rem(s + 1, n), c))
-
-    def halo_up():
-        return send(x_ref, halo.at[1], halo_send.at[1], halo_recv.at[1], (g, lax.rem(s + n - 1, n), c))
-
-    @pl.when(s < n - 1)
-    def _():
-        halo_down().start()
-
-    @pl.when(s > 0)
-    def _():
-        halo_up().start()
 
     def w_copy(k):
         to = lax.rem(s + k, n)
@@ -181,89 +176,94 @@
         w_copy(k).start()
         return 0
 
-    lax.fori_loop(1, n, start_w, 0)
-
-    @pl.when(s > 0)
-    def _():
-        halo_down().wait_recv()
-
-    @pl.when(s == 0)
-    def _():
-        halo[0] = jnp.zeros((tokens, local_ch), jnp.bfloat16)
-
-    @pl.when(s < n - 1)
-    def _():
-        halo_up().wait_recv()
-
-    @pl.when(s == n - 1)
-    def _():
-        halo[1] = jnp.zeros((tokens, local_ch), jnp.bfloat16)
-
-    def conv_part(i, _):
-        cols = pl.ds(pl.multiple_of(i * 128, 128), 128)
-        above = halo[0, :, cols].astype(jnp.float32)
-        here = x_ref[:, cols].astype(jnp.float32)
-        below = halo[1, :, cols].astype(jnp.float32)
-        weight = conv_ref[:, :, cols]
-
-        def column(b):
-            return above * weight[0, b : b + 1] + here * weight[1, b : b + 1] + below * weight[2, b : b + 1]
-
-        token = lax.broadcasted_iota(jnp.int32, (tokens, 128), 0)
-        left = jnp.where(token == 0, 0.0, pltpu.roll(column(0), 1, 0))
-        right = jnp.where(token == tokens - 1, 0.0, pltpu.roll(column(2), tokens - 1, 0))
-        mix[c, :, cols] = (here + (left + column(1) + right)).astype(jnp.bfloat16)
-        return 0
-
-    lax.fori_loop(0, local_ch // 128, conv_part, 0)
-
-    to_peer = send(mix.at[c], mix.at[c], mix_send, mix_recv, other_core)
-    to_peer.start()
-    send(mix.at[1 - c], mix.at[1 - c], mix_send, mix_recv, other_core).wait_recv()
-
-    def norm_part(i, _):
-        rows = pl.ds(pl.multiple_of(i * 16, 16), 16)
-        first = mix[0, rows, :].astype(jnp.float32)
-        second = mix[1, rows, :].astype(jnp.float32)
-        channels = 2 * local_ch
-        mean = (jnp.sum(first, axis=1, keepdims=True) + jnp.sum(second, axis=1, keepdims=True)) / channels
-        first, second = first - mean, second - mean
-        var = (
-            jnp.sum(first * first, axis=1, keepdims=True) + jnp.sum(second * second, axis=1, keepdims=True)
-        ) / channels
-        scale = lax.rsqrt(var + 1e-06)
-        xs[s, 0, rows, :] = (first * scale * gain_ref[:, :local_ch]).astype(jnp.bfloat16)
-        xs[s, 1, rows, :] = (second * scale * gain_ref[:, local_ch:]).astype(jnp.bfloat16)
-        return 0
-
-    lax.fori_loop(0, tokens // 16, norm_part, 0)
-
-    def ring_block(way, k):
+
+    def mix_row(r):
+        def conv_part(i, _):
+            cols = pl.ds(pl.multiple_of(i * 128, 128), 128)
+            above = raw[r, :, cols].astype(jnp.float32)
+            here = raw[r + 1, :, cols].astype(jnp.float32)
+            below = raw[r + 2, :, cols].astype(jnp.float32)
+            weight = conv_ref[:, :, cols]
+
+            def column(b):
+                return above * weight[0, b : b + 1] + here * weight[1, b : b + 1] + below * weight[2, b : b + 1]
+
+            token = lax.broadcasted_iota(jnp.int32, (tokens, 128), 0)
+            left = jnp.where(token == 0, 0.0, pltpu.roll(column(0), 1, 0))
+            right = jnp.where(token == tokens - 1, 0.0, pltpu.roll(column(2), tokens - 1, 0))
+            xs[r, c, :, cols] = (here + (left + column(1) + right)).astype(jnp.bfloat16)
+            return 0
+
+        lax.fori_loop(0, local_ch // 128, conv_part, 0)
+
+        def stat_part(i, _):
+            rows = pl.ds(pl.multiple_of(i * 32, 32), 32)
+            values = xs[r, c, rows, :].astype(jnp.float32)
+            mean = jnp.sum(values, axis=1, keepdims=True) / local_ch
+            values = values - mean
+            spread = jnp.sum(values * values, axis=1, keepdims=True)
+            stats[r, c, 0, rows, :] = jnp.broadcast_to(mean, (32, 128))
+            stats[r, c, 1, rows, :] = jnp.broadcast_to(spread, (32, 128))
+            return 0
+
+        lax.fori_loop(0, tokens // 32, stat_part, 0)
+        stat_copy(r, c).start()
+
+    def stat_copy(r, core):
+        return send(stats.at[r, core], stats.at[r, core], stat_send.at[r], stat_recv.at[r], other_core)
+
+    def row_copy(r, core):
+        return send(xs.at[r, core], xs.at[r, core], peer_send.at[r], peer_recv.at[r], other_core)
+
+    def norm_row(r):
+        stat_copy(r, 1 - c).wait_recv()
+        gain = gain_ref[:, pl.ds(pl.multiple_of(c * local_ch, local_ch), local_ch)]
+
+        def norm_part(i, _):
+            rows = pl.ds(pl.multiple_of(i * 32, 32), 32)
+            mean_0, mean_1 = stats[r, 0, 0, rows, :1], stats[r, 1, 0, rows, :1]
+            gap = mean_0 - mean_1
+            mean = 0.5 * (mean_0 + mean_1)
+            spread = stats[r, 0, 1, rows, :1] + stats[r, 1, 1, rows, :1] + gap * gap * (0.5 * local_ch)
+            scale = lax.rsqrt(spread / (2 * local_ch) + 1e-06)
+            values = xs[r, c, rows, :].astype(jnp.float32)
+            xs[r, c, rows, :] = ((values - mean) * scale * gain).astype(jnp.bfloat16)
+            return 0
+
+        lax.fori_loop(0, tokens // 32, norm_part, 0)
+        row_copy(r, c).start()
+
+    def ring_block(way, k, split):
         owner = at_ring(pos - k if way == 0 else pos + k)
-        if k < half:
-            return xs.at[owner, c]
-        return xs.at[owner, c, pl.ds(way * (tokens // 2), tokens // 2)]
+        if not split:
+            return raw.at[owner + 1]
+        return raw.at[owner + 1, pl.ds(way * (tokens // 2), tokens // 2)]
 
     def ring_copy(way, k):
-        owner = at_ring(pos - (k - 1) if way == 0 else pos + (k - 1))
-        part = xs.at[owner, c] if k < half else xs.at[owner, c, pl.ds(way * (tokens // 2), tokens // 2)]
+        part = ring_block(way, k - 1, k == half)
         to = (g, at_ring(pos + 1 if way == 0 else pos - 1), c)
         return send(part, part, ring_send.at[way, k], ring_recv.at[way, k], to)
 
     def ring_arrived(way, k):
-        part = ring_block(way, k)
+        part = ring_block(way, k, k == half)
         return send(part, part, ring_send.at[way, k], ring_recv.at[way, k], other_core)
 
-    def peer_copy(way, k):
-        part = ring_block(way, k)
-        return send(part, part, peer_send.at[way, k], peer_recv.at[way, k], other_core)
-
-    def peer_arrived(way, k):
-        owner = at_ring(pos - k if way == 0 else pos + k)
-        part = xs.at[owner, 1 - c]
-        if k == half:
-            part = xs.at[owner, 1 - c, pl.ds(way * (tokens // 2), tokens // 2)]
-        return send(part, part, peer_send.at[way, k], peer_recv.at[way, k], other_core)
+    def steps(r):
+        away = lax.rem((r % 2) * (n - 1) + (1 - 2 * (r % 2)) * (r // 2) - pos + n, n)
+        return away + (n - 2 * away) * (away // (half + 1))
+
+    def ready(r):
+        return jnp.maximum(steps(r), jnp.maximum(steps(jnp.maximum(r - 1, 0)), steps(jnp.minimum(r + 1, n - 1))))
+
+    def for_rows(k, act):
+        def one(r, _):
+            @pl.when(ready(r) == k)
+            def _():
+                act(r)
+
+            return 0
+
+        lax.fori_loop(0, n, one, 0)
 
     def project(owner):
         total = []
@@ -278,30 +278,33 @@
         ks[rows, :] = total[1][:, :wide].astype(jnp.bfloat16)
         vs[rows, :] = total[1][:, wide:].astype(jnp.bfloat16)
 
-    def project_pair(k):
-        def one(i, _):
-            project(at_ring(pos - k + 2 * k * i))
-            return 0
-
-        lax.fori_loop(0, 2, one, 0)
-
-    for way in range(2):
-        ring_copy(way, 1).start()
+    def finish_row(r):
+        row_copy(r, 1 - c).wait_recv()
+        project(r)
 
     def forward_w(k, _):
         w_arrived(k).wait_recv()
         w_forward(k).start()
         return 0
 
-    lax.fori_loop(1, n, forward_w, 0)
+
+    own_x.wait()
+    for way in range(2):
+        ring_copy(way, 1).start()
+    lax.fori_loop(1, n, start_w, 0)
+    own_conv.wait()
+    own_gain.wait()
 
     for k in range(1, half + 1):
         for way in range(2):
             ring_arrived(way, k).wait_recv()
             if k < half:
                 ring_copy(way, k + 1).start()
-            peer_copy(way, k).start()
-        if k == 1:
+        for_rows(k, mix_row)
+        if k < 3:
+            lax.fori_loop(1 + (k - 1) * (n - 1) // 2, 1 + k * (n - 1) // 2, forward_w, 0)
+        for_rows(k, norm_row)
+        if k == half:
             own_w.wait()
 
             def w_last(j, _):
@@ -309,14 +312,9 @@
                 return 0
 
             lax.fori_loop(1, n, w_last, 0)
-            project(s)
-        else:
-            for way in range(2):
-                peer_arrived(way, k - 1).wait_recv()
-            project_pair(k - 1)
-    for way in range(2):
-        peer_arrived(way, half).wait_recv()
-    project(at_ring(pos + half))
+            for j in range(1, half):
+                for_rows(j, finish_row)
+    for_rows(half, finish_row)
 
     def out_copy(i):
         to = lax.rem(s + 1 + i, n)
@@ -360,25 +358,22 @@
     lax.fori_loop(0, n, attend_block, 0)
     out_ref[:, pl.ds(pl.multiple_of(s * wide, wide), wide)] = os[n - 1]
 
-    @pl.when(s < n - 1)
-    def _():
-        halo_down().wait_send()
-
-    @pl.when(s > 0)
-    def _():
-        halo_up().wait_send()
-
     def sent_w(k, _):
         w_copy(k).wait_send()
         w_forward(k).wait_send()
         return 0
 
     lax.fori_loop(1, n, sent_w, 0)
-    to_peer.wait_send()
     for k in range(1, half + 1):
         for way in range(2):
             ring_copy(way, k).wait_send()
-            peer_copy(way, k).wait_send()
+
+    def sent_row(r, _):
+        stat_copy(r, c).wait_send()
+        row_copy(r, c).wait_send()
+        return 0
+
+    lax.fori_loop(0, n, sent_row, 0)
 
     def out_done(i, _):
         out_copy(i).wait_send()
@@ -399,23 +394,26 @@
     out = pl.pallas_call(
         functools.partial(fused_kernel, n),
         out_shape=jax.ShapeDtypeStruct((cols, local_ch), jnp.bfloat16),
-        in_specs=[vmem, vmem, vmem, pl.BlockSpec(memory_space=pl.ANY)],
+        in_specs=[pl.BlockSpec(memory_space=pltpu.HBM)] * 4,
         out_specs=vmem,
         scratch_shapes=[
-            pltpu.VMEM((2, cols, local_ch), jnp.bfloat16),
-            pltpu.VMEM((2, cols, local_ch), jnp.bfloat16),
+            pltpu.VMEM(conv_weight.shape, jnp.float32),
+            pltpu.VMEM((1, D), jnp.float32),
+            dma((3,)),
+            pltpu.VMEM((n + 2, cols, local_ch), jnp.bfloat16),
+            pltpu.VMEM((n, 2, 2, cols, 128), jnp.float32),
             pltpu.VMEM((n, 2, cols, local_ch), jnp.bfloat16),
             pltpu.VMEM((3, n * depth, wide), jnp.bfloat16),
             pltpu.VMEM((count, wide), jnp.bfloat16),
             pltpu.VMEM((count, wide), jnp.bfloat16),
             pltpu.VMEM((count, wide), jnp.bfloat16),
             pltpu.VMEM((n, cols, wide), jnp.bfloat16),
-            dma((2,)), dma((2,)), dma, dma((n,)), dma((n,)), dma((n,)), dma((n,)), dma, dma,
-            dma((2, half + 1)), dma((2, half + 1)), dma((2, half + 1)), dma((2, half + 1)),
+            dma, dma((n,)), dma((n,)), dma((n,)), dma((n,)), dma((n,)), dma((n,)),
+            dma((2, half + 1)), dma((2, half + 1)), dma((n,)), dma((n,)),
             dma((n,)), dma((n,)),
         ],
         compiler_params=pltpu.CompilerParams(
-            collective_id=0, has_side_effects=True, vmem_limit_bytes=40 * 1024 * 1024
+            collective_id=0, has_side_effects=True, vmem_limit_bytes=63 * 1024 * 1024
         ),
     )(
         grid_tokens.reshape(cols, local_ch), conv_weight, norm_gain.reshape(1, D),

time: 73.6 us -> 70.7 us (0.961)
  local copies, waits for them, and re-layouts: 4.56 us -> 1.67 us
    unnamed x9 -> x1, local copies, waits for them, and re-layouts: 4.56 us -> 1.67 us
where the time goes in v3:
time: 70.7 us; the launch traced here: 70.6 us
  Pallas kernels  68.9 us (97%)
  local copies, waits for them, and re-layouts  1.67 us (2%)
    pallas_call x1, Pallas kernels, local_fused(): pl.pallas_call(functools.partial(fused_kernel, n), out_shape=jax.ShapeDty...  68.9 us
    unnamed x1, local copies, waits for them, and re-layouts  1.67 us

profile of v3, /device:TPU:0, one launch (start us, length us, event | category | flops | bytes accessed | tf_op | source)
XLA Modules:
  0.0 70.6 jit_solution(1512051605211163043)
XLA Ops:
  0.0 68.9 %shard_map.46 = bf16[128,1024]{1,0:T(8,128)(2,1)} custom-call(bf16[128,1024]{1,0:T(8,128)(2,1)} %bitcast.6, f32[3,3,1024]{2,1,0:T(4,128)} %conv_in.1, f32[1,2048]{1,0:T(1,128)} %bitcast.7, bf16[3,256,1024]{2,1,0:T(8,128)(2,1)} %bitcast.4), custom_call_target="tpu_custom_call" | custom-call | tf_op jit(solution)/shard_map/pallas_call | solution.py:394
  68.9 1.7 %copy.6 = bf16[1,128,1024]{2,1,0:T(8,128)(2,1)} copy(bf16[1,128,1024]{2,1,0:T(8,128)(2,1)} %bitcast.5) | data formatting | bytes 524288

commit v4 on v3

--- a/solution.py
+++ b/solution.py
@@ -194,7 +194,7 @@
             xs[r, c, :, cols] = (here + (left + column(1) + right)).astype(jnp.bfloat16)
             return 0
 
-        lax.fori_loop(0, local_ch // 128, conv_part, 0)
+        lax.fori_loop(0, local_ch // 128, conv_part, 0, unroll=2)
 
         def stat_part(i, _):
             rows = pl.ds(pl.multiple_of(i * 32, 32), 32)
@@ -206,7 +206,7 @@
             stats[r, c, 1, rows, :] = jnp.broadcast_to(spread, (32, 128))
             return 0
 
-        lax.fori_loop(0, tokens // 32, stat_part, 0)
+        lax.fori_loop(0, tokens // 32, stat_part, 0, unroll=2)
         stat_copy(r, c).start()
 
     def stat_copy(r, core):
@@ -230,7 +230,7 @@
             xs[r, c, rows, :] = ((values - mean) * scale * gain).astype(jnp.bfloat16)
             return 0
 
-        lax.fori_loop(0, tokens // 32, norm_part, 0)
+        lax.fori_loop(0, tokens // 32, norm_part, 0, unroll=2)
         row_copy(r, c).start()
 
     def ring_block(way, k, split):

time: 70.7 us -> 68.1 us (0.963)
  Pallas kernels: 68.9 us -> 66.3 us
    pallas_call x1, Pallas kernels: 68.9 us -> 66.3 us  [local_fused(): pl.pallas_call(functools.partial(fused_kernel, n), out_shape=jax.ShapeDty...]
where the time goes in v4:
time: 68.1 us; the launch traced here: 68 us
  Pallas kernels  66.3 us (97%)
  local copies, waits for them, and re-layouts  1.67 us (2%)
    pallas_call x1, Pallas kernels, local_fused(): pl.pallas_call(functools.partial(fused_kernel, n), out_shape=jax.ShapeDty...  66.3 us
    unnamed x1, local copies, waits for them, and re-layouts  1.67 us

profile of v4, /device:TPU:0, one launch (start us, length us, event | category | flops | bytes accessed | tf_op | source)
XLA Modules:
  0.0 68.0 jit_solution(13523618421974880183)
XLA Ops:
  0.0 66.3 %shard_map.46 = bf16[128,1024]{1,0:T(8,128)(2,1)} custom-call(bf16[128,1024]{1,0:T(8,128)(2,1)} %bitcast.6, f32[3,3,1024]{2,1,0:T(4,128)} %conv_in.1, f32[1,2048]{1,0:T(1,128)} %bitcast.7, bf16[3,256,1024]{2,1,0:T(8,128)(2,1)} %bitcast.4), custom_call_target="tpu_custom_call" | custom-call | tf_op jit(solution)/shard_map/pallas_call | solution.py:394
  66.3 1.7 %copy.6 = bf16[1,128,1024]{2,1,0:T(8,128)(2,1)} copy(bf16[1,128,1024]{2,1,0:T(8,128)(2,1)} %bitcast.5) | data formatting | bytes 524288
